TPU v7x, 32 devices: a whole 2x2x4 slice. The times are simulated.
32 devices in a mesh: grp: 2 (over y), lon: 4 (over z), lat: 2 (over x), dir: 2 (over core).
Axes of the slice: x: 2, y: 2, z: 4, core: 2. Of those that a mesh axis runs over, the one named last changes fastest.
Arguments:
- perturb: float32 [6, 16, 64, 512], P('grp', 'dir', 'lat', 'lon'), parts along dimension 0, may hold values from -6 to 6
- background: float32 [6, 64, 512], P('grp', 'lat', 'lon'), parts along dimension 0, may hold values from -0.3 to 0.3
- land_mask: int32 [64, 512], P('lat', 'lon'), may hold values 0 or 1
- levels: int32 [64, 512], P('lat', 'lon'), may hold values from 1 to 90
- fold_partner: int32 [512], replicated, may hold values from 0 to 511, as said below
Outputs:
- evolved: float32 [6, 16, 64, 512], P('grp', 'dir', 'lat', 'lon'), parts along dimension 0
There are 2 independent parts, one for each index of `grp`. A program takes and returns all parts, laid end to end along the dimension named above; an argument that names none is the same for every part. Nothing has to cross between parts.
Inputs may be any that keep to these rules, and one draw needn't show every extreme that they name: fold_partner[i] = (P - i) mod 512 for one odd P of the draw.
All inputs are finite; a program needn't handle non-finite values. No bound on the sum of `land_mask` on one device may be relied on, other than what follows from the above.
Results may differ from a plain program's by a relative error of at most 0.00002.
Values sent between devices are 32-bit elements; how exact they have to be, the bound alone decides.
No kernel may reach another device: no remote copies, remote signals or barrier semaphores. Data moves between devices by JAX's collectives and lax.ppermute only.
A program may use at most 64 MiB of HBM per device.

v0:
```python
import jax
import jax.numpy as jnp
from jax import lax
from jax.sharding import PartitionSpec as P

SUBCYCLES = 5
NLEV = 90


TIME_STEP = 0.35


def with_halo(x, sides, width, wrap):
    for axis, dim in sides:
        size, length = (lax.axis_size(axis), x.shape[dim])
        up = [(i, (i + 1) % size) for i in range(size if wrap else size - 1)]
        down = [(j, i) for i, j in up]
        last = lax.slice_in_dim(x, length - width, length, axis=dim)
        first = lax.slice_in_dim(x, 0, width, axis=dim)
        before = lax.ppermute(last, axis, up)
        after = lax.ppermute(first, axis, down)
        x = jnp.concatenate([before, x, after], axis=dim)
    return x


def extend(fields, signs, width, partner):
    height = fields.shape[2]
    breadth = fields.shape[3]
    grown = with_halo(fields, (("lat", 2),), width, False)
    edge_rows = jnp.flip(fields[:, :, height - width :, :], axis=2)
    first_col = lax.axis_index("lon") * breadth
    whole_rows = lax.all_gather(edge_rows, "lon", axis=3, tiled=True)
    facing = lax.dynamic_slice_in_dim(partner, first_col, breadth)
    mirror = jnp.take(whole_rows, facing, axis=3) * signs
    at_top = lax.axis_index("lat") == lax.axis_size("lat") - 1
    northern = jnp.where(at_top, mirror, grown[:, :, height + width :, :])
    grown = jnp.concatenate([grown[:, :, : height + width, :], northern], axis=2)
    return with_halo(grown, (("lon", 3),), width, True)


def on_device(perturb, background, land_mask, levels, fold_partner):
    height = perturb.shape[2]
    wet_cells = land_mask.astype(jnp.float32)
    depth = 0.5 + 1.5 * ((levels - 1).astype(jnp.float32) / (NLEV - 1)) ** 2
    thickness = wet_cells * (depth + background[0])
    coef_signs = jnp.array([1.0, -1.0, -1.0, 1.0], jnp.float32).reshape(4, 1, 1, 1)
    state_signs = jnp.array([1.0, -1.0, -1.0], jnp.float32).reshape(3, 1, 1, 1)
    elev_sign = jnp.ones((1, 1, 1, 1), jnp.float32)
    coeffs = jnp.stack([thickness, background[1], background[2], wet_cells])[:, None]
    wide = extend(coeffs, coef_signs, 2, fold_partner)
    grid_rows = (lax.axis_index("lat") * height + jnp.arange(height, dtype=jnp.int32)).astype(
        jnp.float32
    )
    all_rows = height * lax.axis_size("lat")
    coriolis = (0.3 + 0.2 * grid_rows / all_rows)[:, None]
    elevation, zonal, meridional = (perturb[0], perturb[1], perturb[2])
    for subcycle in range(SUBCYCLES):
        narrow = wide[:, :, 1:-1, 1:-1]
        grown = extend(jnp.stack([elevation, zonal, meridional]), state_signs, 1, fold_partner)
        flux_east = narrow[0] * grown[1] + grown[0] * narrow[1]
        flux_north = narrow[0] * grown[2] + grown[0] * narrow[2]
        divergence = 0.5 * (flux_east[:, 1:-1, 2:] - flux_east[:, 1:-1, :-2]) + 0.5 * (
            flux_north[:, 2:, 1:-1] - flux_north[:, :-2, 1:-1]
        )
        elevation = wet_cells * (elevation - TIME_STEP * divergence)
        ext_elev = extend(elevation[None], elev_sign, 1, fold_partner)[0]
        slope_east = 0.5 * (ext_elev[:, 1:-1, 2:] - ext_elev[:, 1:-1, :-2])
        slope_north = 0.5 * (ext_elev[:, 2:, 1:-1] - ext_elev[:, :-2, 1:-1])
        zonal = wet_cells * (zonal + TIME_STEP * (coriolis * meridional - slope_east))
        meridional = wet_cells * (meridional - TIME_STEP * (coriolis * zonal + slope_north))
    return jnp.stack([elevation, zonal, meridional])


def solution(mesh):
    placed = (
        P("grp", "dir", "lat", "lon"),
        P("grp", "lat", "lon"),
        P("lat", "lon"),
        P("lat", "lon"),
        P(),
    )
    return jax.shard_map(
        on_device,
        mesh=mesh,
        in_specs=placed,
        out_specs=P("grp", "dir", "lat", "lon"),
        check_vma=False,
    )
```

profile of v0, /device:TPU:0, one launch (start us, length us, event | category | flops | bytes accessed | tf_op | source)
XLA Modules:
  0.0 338.9 jit_solution(18149557243043410009)
XLA Ops:
  2.3 1.9 copy.434
  4.3 1.3 collective-permute-start.1
  5.6 4.9 %collective-permute-start = (f32[4,1,2,128]{0,2,3,1:T(2,128)S(1)}, f32[4,1,2,128]{0,2,3,1:T(2,128)S(1)}, u32[]{:S(2)}, u32[]{:S(2)}) collective-permute-start(f32[4,1,2,128]{0,2,3,1:T(2,128)S(1)} %get-tuple-element.17), channel_id=1, source_target_pairs={{0,2},{1,3},{4,6},{5,7},{8,10},{9,11},{12,14},{13,15},{16,18},{17,... | collective-permute-start | bytes 12296 | tf_op jit(solution)/shard_map/ppermute | solution.py:20
  10.5 1.3 collective-permute-start.5
  12.1 4.5 %collective-permute-start.4 = (f32[3,8,1,128]{3,1,2,0:T(8,128)S(1)}, f32[3,8,1,128]{3,1,2,0:T(8,128)S(1)}, u32[]{:S(2)}, u32[]{:S(2)}) collective-permute-start(f32[3,8,1,128]{3,1,2,0:T(8,128)S(1)} %slice.498), channel_id=1, source_target_pairs={{0,2},{1,3},{4,6},{5,7},{8,10},{9,11},{12,14},{13,15},{16,18},{17,... | collective-permute-start | bytes 36872 | tf_op jit(solution)/shard_map/ppermute | solution.py:20
  17.8 13.3 %all_gather.33 = f32[4,1,2,512]{3,0,2,1:T(4,128)S(1)} all-gather(f32[4,1,2,128]{3,0,2,1:T(4,128)S(1)} %copy.435), channel_id=1, replica_groups=mesh['grp'=2,'lon'=4,'lat'=2,'dir'=2] {'lon'}, dimensions={3}, use_global_device_ids=true | all-gather | bytes 20480 | tf_op jit(solution)/shard_map/all_gather | solution.py:32
  32.7 1.6 collective-permute-start.2
  34.3 2.3 collective-permute-start.3
  36.5 13.3 %all_gather.34 = f32[3,8,1,512]{3,1,2,0:T(8,128)S(1)} all-gather(f32[3,8,1,128]{3,1,2,0:T(8,128)S(1)} %slice.498), channel_id=1, replica_groups=mesh['grp'=2,'lon'=4,'lat'=2,'dir'=2] {'lon'}, dimensions={3}, use_global_device_ids=true | all-gather | bytes 61440 | tf_op jit(solution)/shard_map/all_gather | solution.py:32
  52.0 3.8 %collective-permute-start.7 = (f32[3,8,34,1]{3,1,2,0:T(8,128)S(1)}, f32[3,8,34,1]{3,1,2,0:T(8,128)S(1)}, u32[]{:S(2)}, u32[]{:S(2)}) collective-permute-start(f32[3,8,34,1]{3,1,2,0:T(8,128)S(1)} %get-tuple-element.45), channel_id=1, source_target_pairs={{4,0},{8,4},{12,8},{0,12},{5,1},{9,5},{13,9},{1,13},{6,2},{10,6},{... | collective-permute-start | bytes 9800 | tf_op jit(solution)/shard_map/ppermute | solution.py:21
  55.8 6.7 %collective-permute-done.6 = f32[3,8,34,1]{3,1,2,0:T(8,128)S(1)} collective-permute-done((f32[3,8,34,1]{3,1,2,0:T(8,128)S(1)}, f32[3,8,34,1]{3,1,2,0:T(8,128)S(1)}, u32[]{:S(2)}, u32[]{:S(2)}) %collective-permute-start.6) | collective-permute-done | bytes 3296 | tf_op jit(solution)/shard_map/ppermute | solution.py:20
  62.5 2.6 collective-permute-done.7
  66.1 1.3 collective-permute-start.9
  67.4 4.5 %collective-permute-start.8 = (f32[1,8,1,128]{3,2,1,0:T(1,128)S(1)}, f32[1,8,1,128]{3,2,1,0:T(1,128)S(1)}, u32[]{:S(2)}, u32[]{:S(2)}) collective-permute-start(f32[1,8,1,128]{3,2,1,0:T(1,128)S(1)} %get-tuple-element.85), channel_id=1, source_target_pairs={{0,2},{1,3},{4,6},{5,7},{8,10},{9,11},{12,14},{13,15},{16,18},{17,... | collective-permute-start | bytes 12296 | tf_op jit(solution)/shard_map/ppermute | solution.py:20
  72.0 9.8 %all_gather.35 = f32[1,8,1,512]{3,2,1,0:T(1,128)S(1)} all-gather(f32[1,8,1,128]{3,2,1,0:T(1,128)S(1)} %get-tuple-element.85), channel_id=1, replica_groups=mesh['grp'=2,'lon'=4,'lat'=2,'dir'=2] {'lon'}, dimensions={3}, use_global_device_ids=true | all-gather | bytes 20480 | tf_op jit(solution)/shard_map/all_gather | solution.py:32
  82.8 3.8 %collective-permute-start.11 = (f32[1,8,34,1]{3,1,2,0:T(8,128)S(1)}, f32[1,8,34,1]{3,1,2,0:T(8,128)S(1)}, u32[]{:S(2)}, u32[]{:S(2)}) collective-permute-start(f32[1,8,34,1]{3,1,2,0:T(8,128)S(1)} %get-tuple-element.76), channel_id=1, source_target_pairs={{4,0},{8,4},{12,8},{0,12},{5,1},{9,5},{13,9},{1,13},{6,2},{10,6},{... | collective-permute-start | bytes 3272 | tf_op jit(solution)/shard_map/ppermute | solution.py:21
  86.7 3.2 collective-permute-done.10
  90.6 1.3 collective-permute-start.13
  91.9 4.5 %collective-permute-start.12 = (f32[3,8,1,128]{3,2,1,0:T(1,128)S(1)}, f32[3,8,1,128]{3,2,1,0:T(1,128)S(1)}, u32[]{:S(2)}, u32[]{:S(2)}) collective-permute-start(f32[3,8,1,128]{3,2,1,0:T(1,128)S(1)} %get-tuple-element.52), channel_id=1, source_target_pairs={{0,2},{1,3},{4,6},{5,7},{8,10},{9,11},{12,14},{13,15},{16,18},{17,... | collective-permute-start | bytes 36872 | tf_op jit(solution)/shard_map/ppermute | solution.py:20
  96.5 16.1 %all_gather.36 = f32[3,8,1,512]{3,1,2,0:T(8,128)S(1)} all-gather(f32[3,8,1,128]{3,1,2,0:T(8,128)S(1)} %bitcast.296), channel_id=1, replica_groups=mesh['grp'=2,'lon'=4,'lat'=2,'dir'=2] {'lon'}, dimensions={3}, use_global_device_ids=true | all-gather | bytes 61440 | tf_op jit(solution)/shard_map/all_gather | solution.py:32
  114.2 3.8 %collective-permute-start.15 = (f32[3,8,34,1]{3,1,2,0:T(8,128)S(1)}, f32[3,8,34,1]{3,1,2,0:T(8,128)S(1)}, u32[]{:S(2)}, u32[]{:S(2)}) collective-permute-start(f32[3,8,34,1]{3,1,2,0:T(8,128)S(1)} %get-tuple-element.43), channel_id=1, source_target_pairs={{4,0},{8,4},{12,8},{0,12},{5,1},{9,5},{13,9},{1,13},{6,2},{10,6},{... | collective-permute-start | bytes 9800 | tf_op jit(solution)/shard_map/ppermute | solution.py:21
  118.0 6.3 %collective-permute-done.14 = f32[3,8,34,1]{3,1,2,0:T(8,128)S(1)} collective-permute-done((f32[3,8,34,1]{3,1,2,0:T(8,128)S(1)}, f32[3,8,34,1]{3,1,2,0:T(8,128)S(1)}, u32[]{:S(2)}, u32[]{:S(2)}) %collective-permute-start.14) | collective-permute-done | bytes 3296 | tf_op jit(solution)/shard_map/ppermute | solution.py:20
  124.3 2.6 collective-permute-done.15
  128.0 1.3 collective-permute-start.17
  129.3 4.5 %collective-permute-start.16 = (f32[1,8,1,128]{3,2,1,0:T(1,128)S(1)}, f32[1,8,1,128]{3,2,1,0:T(1,128)S(1)}, u32[]{:S(2)}, u32[]{:S(2)}) collective-permute-start(f32[1,8,1,128]{3,2,1,0:T(1,128)S(1)} %get-tuple-element.83), channel_id=1, source_target_pairs={{0,2},{1,3},{4,6},{5,7},{8,10},{9,11},{12,14},{13,15},{16,18},{17,... | collective-permute-start | bytes 12296 | tf_op jit(solution)/shard_map/ppermute | solution.py:20
  133.8 9.5 %all_gather.37 = f32[1,8,1,512]{3,2,1,0:T(1,128)S(1)} all-gather(f32[1,8,1,128]{3,2,1,0:T(1,128)S(1)} %get-tuple-element.83), channel_id=1, replica_groups=mesh['grp'=2,'lon'=4,'lat'=2,'dir'=2] {'lon'}, dimensions={3}, use_global_device_ids=true | all-gather | bytes 20480 | tf_op jit(solution)/shard_map/all_gather | solution.py:32
  144.5 3.7 %collective-permute-start.19 = (f32[1,8,34,1]{3,1,2,0:T(8,128)S(1)}, f32[1,8,34,1]{3,1,2,0:T(8,128)S(1)}, u32[]{:S(2)}, u32[]{:S(2)}) collective-permute-start(f32[1,8,34,1]{3,1,2,0:T(8,128)S(1)} %get-tuple-element.74), channel_id=1, source_target_pairs={{4,0},{8,4},{12,8},{0,12},{5,1},{9,5},{13,9},{1,13},{6,2},{10,6},{... | collective-permute-start | bytes 3272 | tf_op jit(solution)/shard_map/ppermute | solution.py:21
  148.2 3.0 collective-permute-done.18
  152.0 1.3 collective-permute-start.21
  153.3 4.5 %collective-permute-start.20 = (f32[3,8,1,128]{3,2,1,0:T(1,128)S(1)}, f32[3,8,1,128]{3,2,1,0:T(1,128)S(1)}, u32[]{:S(2)}, u32[]{:S(2)}) collective-permute-start(f32[3,8,1,128]{3,2,1,0:T(1,128)S(1)} %get-tuple-element.50), channel_id=1, source_target_pairs={{0,2},{1,3},{4,6},{5,7},{8,10},{9,11},{12,14},{13,15},{16,18},{17,... | collective-permute-start | bytes 36872 | tf_op jit(solution)/shard_map/ppermute | solution.py:20
  157.9 13.5 %all_gather.38 = f32[3,8,1,512]{3,1,2,0:T(8,128)S(1)} all-gather(f32[3,8,1,128]{3,1,2,0:T(8,128)S(1)} %bitcast.297), channel_id=1, replica_groups=mesh['grp'=2,'lon'=4,'lat'=2,'dir'=2] {'lon'}, dimensions={3}, use_global_device_ids=true | all-gather | bytes 61440 | tf_op jit(solution)/shard_map/all_gather | solution.py:32
  172.9 2.1 collective-permute-start.22
  175.0 2.1 collective-permute-start.23
  177.1 7.3 %collective-permute-done.22 = f32[3,8,34,1]{3,1,2,0:T(8,128)S(1)} collective-permute-done((f32[3,8,34,1]{3,1,2,0:T(8,128)S(1)}, f32[3,8,34,1]{3,1,2,0:T(8,128)S(1)}, u32[]{:S(2)}, u32[]{:S(2)}) %collective-permute-start.22) | collective-permute-done | bytes 3296 | tf_op jit(solution)/shard_map/ppermute | solution.py:20
  184.3 6.0 %collective-permute-done.23 = f32[3,8,34,1]{3,1,2,0:T(8,128)S(1)} collective-permute-done((f32[3,8,34,1]{3,1,2,0:T(8,128)S(1)}, f32[3,8,34,1]{3,1,2,0:T(8,128)S(1)}, u32[]{:S(2)}, u32[]{:S(2)}) %collective-permute-start.23) | collective-permute-done | bytes 3296 | tf_op jit(solution)/shard_map/ppermute | solution.py:21
  191.3 1.3 collective-permute-start.25
  192.6 4.5 %collective-permute-start.24 = (f32[1,8,1,128]{3,2,1,0:T(1,128)S(1)}, f32[1,8,1,128]{3,2,1,0:T(1,128)S(1)}, u32[]{:S(2)}, u32[]{:S(2)}) collective-permute-start(f32[1,8,1,128]{3,2,1,0:T(1,128)S(1)} %get-tuple-element.81), channel_id=1, source_target_pairs={{0,2},{1,3},{4,6},{5,7},{8,10},{9,11},{12,14},{13,15},{16,18},{17,... | collective-permute-start | bytes 12296 | tf_op jit(solution)/shard_map/ppermute | solution.py:20
  197.2 9.7 %all_gather.39 = f32[1,8,1,512]{3,2,1,0:T(1,128)S(1)} all-gather(f32[1,8,1,128]{3,2,1,0:T(1,128)S(1)} %get-tuple-element.81), channel_id=1, replica_groups=mesh['grp'=2,'lon'=4,'lat'=2,'dir'=2] {'lon'}, dimensions={3}, use_global_device_ids=true | all-gather | bytes 20480 | tf_op jit(solution)/shard_map/all_gather | solution.py:32
  207.9 3.8 %collective-permute-start.27 = (f32[1,8,34,1]{3,1,2,0:T(8,128)S(1)}, f32[1,8,34,1]{3,1,2,0:T(8,128)S(1)}, u32[]{:S(2)}, u32[]{:S(2)}) collective-permute-start(f32[1,8,34,1]{3,1,2,0:T(8,128)S(1)} %get-tuple-element.72), channel_id=1, source_target_pairs={{4,0},{8,4},{12,8},{0,12},{5,1},{9,5},{13,9},{1,13},{6,2},{10,6},{... | collective-permute-start | bytes 3272 | tf_op jit(solution)/shard_map/ppermute | solution.py:21
  211.7 4.6 %collective-permute-done.26 = f32[1,8,34,1]{3,1,2,0:T(8,128)S(1)} collective-permute-done((f32[1,8,34,1]{3,1,2,0:T(8,128)S(1)}, f32[1,8,34,1]{3,1,2,0:T(8,128)S(1)}, u32[]{:S(2)}, u32[]{:S(2)}) %collective-permute-start.26) | collective-permute-done | bytes 1120 | tf_op jit(solution)/shard_map/ppermute | solution.py:20
  216.3 2.7 collective-permute-done.27
  219.7 1.3 collective-permute-start.29
  221.0 4.5 %collective-permute-start.28 = (f32[3,8,1,128]{3,2,1,0:T(1,128)S(1)}, f32[3,8,1,128]{3,2,1,0:T(1,128)S(1)}, u32[]{:S(2)}, u32[]{:S(2)}) collective-permute-start(f32[3,8,1,128]{3,2,1,0:T(1,128)S(1)} %get-tuple-element.48), channel_id=1, source_target_pairs={{0,2},{1,3},{4,6},{5,7},{8,10},{9,11},{12,14},{13,15},{16,18},{17,... | collective-permute-start | bytes 36872 | tf_op jit(solution)/shard_map/ppermute | solution.py:20
  225.6 13.2 %all_gather.40 = f32[3,8,1,512]{3,1,2,0:T(8,128)S(1)} all-gather(f32[3,8,1,128]{3,1,2,0:T(8,128)S(1)} %bitcast.298), channel_id=1, replica_groups=mesh['grp'=2,'lon'=4,'lat'=2,'dir'=2] {'lon'}, dimensions={3}, use_global_device_ids=true | all-gather | bytes 61440 | tf_op jit(solution)/shard_map/all_gather | solution.py:32
  240.4 3.8 %collective-permute-start.31 = (f32[3,8,34,1]{3,1,2,0:T(8,128)S(1)}, f32[3,8,34,1]{3,1,2,0:T(8,128)S(1)}, u32[]{:S(2)}, u32[]{:S(2)}) collective-permute-start(f32[3,8,34,1]{3,1,2,0:T(8,128)S(1)} %get-tuple-element.39), channel_id=1, source_target_pairs={{4,0},{8,4},{12,8},{0,12},{5,1},{9,5},{13,9},{1,13},{6,2},{10,6},{... | collective-permute-start | bytes 9800 | tf_op jit(solution)/shard_map/ppermute | solution.py:21
  244.2 6.2 %collective-permute-done.30 = f32[3,8,34,1]{3,1,2,0:T(8,128)S(1)} collective-permute-done((f32[3,8,34,1]{3,1,2,0:T(8,128)S(1)}, f32[3,8,34,1]{3,1,2,0:T(8,128)S(1)}, u32[]{:S(2)}, u32[]{:S(2)}) %collective-permute-start.30) | collective-permute-done | bytes 3296 | tf_op jit(solution)/shard_map/ppermute | solution.py:20
  250.4 2.7 collective-permute-done.31
  254.1 1.3 collective-permute-start.33
  255.4 4.5 %collective-permute-start.32 = (f32[1,8,1,128]{3,2,1,0:T(1,128)S(1)}, f32[1,8,1,128]{3,2,1,0:T(1,128)S(1)}, u32[]{:S(2)}, u32[]{:S(2)}) collective-permute-start(f32[1,8,1,128]{3,2,1,0:T(1,128)S(1)} %get-tuple-element.79), channel_id=1, source_target_pairs={{0,2},{1,3},{4,6},{5,7},{8,10},{9,11},{12,14},{13,15},{16,18},{17,... | collective-permute-start | bytes 12296 | tf_op jit(solution)/shard_map/ppermute | solution.py:20
  260.0 9.7 %all_gather.41 = f32[1,8,1,512]{3,2,1,0:T(1,128)S(1)} all-gather(f32[1,8,1,128]{3,2,1,0:T(1,128)S(1)} %get-tuple-element.79), channel_id=1, replica_groups=mesh['grp'=2,'lon'=4,'lat'=2,'dir'=2] {'lon'}, dimensions={3}, use_global_device_ids=true | all-gather | bytes 20480 | tf_op jit(solution)/shard_map/all_gather | solution.py:32
  270.6 2.0 collective-permute-start.34
  272.6 1.9 collective-permute-start.35
  274.5 3.2 collective-permute-done.34
  277.7 1.3 collective-permute-done.35
  281.1 4.5 %collective-permute-start.36 = (f32[3,8,1,128]{3,2,1,0:T(1,128)S(1)}, f32[3,8,1,128]{3,2,1,0:T(1,128)S(1)}, u32[]{:S(2)}, u32[]{:S(2)}) collective-permute-start(f32[3,8,1,128]{3,2,1,0:T(1,128)S(1)} %get-tuple-element.46), channel_id=1, source_target_pairs={{0,2},{1,3},{4,6},{5,7},{8,10},{9,11},{12,14},{13,15},{16,18},{17,... | collective-permute-start | bytes 36872 | tf_op jit(solution)/shard_map/ppermute | solution.py:20
  285.7 13.1 %all_gather.42 = f32[3,8,1,512]{3,1,2,0:T(8,128)S(1)} all-gather(f32[3,8,1,128]{3,1,2,0:T(8,128)S(1)} %bitcast.295), channel_id=1, replica_groups=mesh['grp'=2,'lon'=4,'lat'=2,'dir'=2] {'lon'}, dimensions={3}, use_global_device_ids=true | all-gather | bytes 61440 | tf_op jit(solution)/shard_map/all_gather | solution.py:32
  300.9 3.4 collective-permute-start.39
  304.3 6.2 %collective-permute-done.38 = f32[3,8,34,1]{3,1,2,0:T(8,128)S(1)} collective-permute-done((f32[3,8,34,1]{3,1,2,0:T(8,128)S(1)}, f32[3,8,34,1]{3,1,2,0:T(8,128)S(1)}, u32[]{:S(2)}, u32[]{:S(2)}) %collective-permute-start.38) | collective-permute-done | bytes 3296 | tf_op jit(solution)/shard_map/ppermute | solution.py:20
  310.4 3.0 collective-permute-done.39
  314.4 1.3 collective-permute-start.41
  315.7 4.5 %collective-permute-start.40 = (f32[1,8,1,128]{3,2,1,0:T(1,128)S(1)}, f32[1,8,1,128]{3,2,1,0:T(1,128)S(1)}, u32[]{:S(2)}, u32[]{:S(2)}) collective-permute-start(f32[1,8,1,128]{3,2,1,0:T(1,128)S(1)} %get-tuple-element.77), channel_id=1, source_target_pairs={{0,2},{1,3},{4,6},{5,7},{8,10},{9,11},{12,14},{13,15},{16,18},{17,... | collective-permute-start | bytes 12296 | tf_op jit(solution)/shard_map/ppermute | solution.py:20
  320.3 9.5 %all_gather.43 = f32[1,8,1,512]{3,2,1,0:T(1,128)S(1)} all-gather(f32[1,8,1,128]{3,2,1,0:T(1,128)S(1)} %get-tuple-element.77), channel_id=1, replica_groups=mesh['grp'=2,'lon'=4,'lat'=2,'dir'=2] {'lon'}, dimensions={3}, use_global_device_ids=true | all-gather | bytes 20480 | tf_op jit(solution)/shard_map/all_gather | solution.py:32
  331.0 3.6 %collective-permute-start.43 = (f32[1,8,34,1]{3,1,2,0:T(8,128)S(1)}, f32[1,8,34,1]{3,1,2,0:T(8,128)S(1)}, u32[]{:S(2)}, u32[]{:S(2)}) collective-permute-start(f32[1,8,34,1]{3,1,2,0:T(8,128)S(1)} %get-tuple-element.68), channel_id=1, source_target_pairs={{4,0},{8,4},{12,8},{0,12},{5,1},{9,5},{13,9},{1,13},{6,2},{10,6},{... | collective-permute-start | bytes 3272 | tf_op jit(solution)/shard_map/ppermute | solution.py:21
  334.7 3.0 collective-permute-done.42
  (184 shorter events, 30.1 us)
Async XLA Ops:
  0.0 10.5 %copy-start = (f32[3,8,32,128]{3,2,1,0:T(8,128)S(1)}, f32[3,8,32,128]{3,2,1,0:T(8,128)}, u32[]{:S(2)}) copy-start(f32[3,8,32,128]{3,2,1,0:T(8,128)} %param.11) | copy-start | bytes 1179652
  2.3 29.8 %copy-start.2 = (f32[4]{0:T(128)S(1)}, f32[4]{0:T(128)}, u32[]{:S(2)}) copy-start(f32[4]{0:T(128)} %constant.83.clone) | copy-start | bytes 52
  4.3 27.8 %collective-permute-start.1 = (f32[4,1,2,128]{0,2,3,1:T(2,128)S(1)}, f32[4,1,2,128]{0,2,3,1:T(2,128)S(1)}, u32[]{:S(2)}, u32[]{:S(2)}) collective-permute-start(f32[4,1,2,128]{0,2,3,1:T(2,128)S(1)} %get-tuple-element.18), channel_id=1, source_target_pairs={{2,0},{3,1},{6,4},{7,5},{10,8},{11,9},{14,12},{15,13},{18,16},{19,... | collective-permute-start | bytes 12296 | tf_op jit(solution)/shard_map/ppermute | solution.py:21
  5.6 26.8 %collective-permute-start = (f32[4,1,2,128]{0,2,3,1:T(2,128)S(1)}, f32[4,1,2,128]{0,2,3,1:T(2,128)S(1)}, u32[]{:S(2)}, u32[]{:S(2)}) collective-permute-start(f32[4,1,2,128]{0,2,3,1:T(2,128)S(1)} %get-tuple-element.17), channel_id=1, source_target_pairs={{0,2},{1,3},{4,6},{5,7},{8,10},{9,11},{12,14},{13,15},{16,18},{17,... | collective-permute-start | bytes 12296 | tf_op jit(solution)/shard_map/ppermute | solution.py:20
  10.5 41.1 %collective-permute-start.5 = (f32[3,8,1,128]{3,2,1,0:T(1,128)S(1)}, f32[3,8,1,128]{3,2,1,0:T(1,128)S(1)}, u32[]{:S(2)}, u32[]{:S(2)}) collective-permute-start(f32[3,8,1,128]{3,2,1,0:T(1,128)S(1)} %slice.374), channel_id=1, source_target_pairs={{2,0},{3,1},{6,4},{7,5},{10,8},{11,9},{14,12},{15,13},{18,16},{19,... | collective-permute-start | bytes 36872 | tf_op jit(solution)/shard_map/ppermute | solution.py:21
  12.0 39.6 %copy-start.1 = (f32[3]{0:T(128)S(1)}, f32[3]{0:T(128)}, u32[]{:S(2)}) copy-start(f32[3]{0:T(128)} %constant.84.clone) | copy-start | bytes 40
  12.1 39.6 %collective-permute-start.4 = (f32[3,8,1,128]{3,1,2,0:T(8,128)S(1)}, f32[3,8,1,128]{3,1,2,0:T(8,128)S(1)}, u32[]{:S(2)}, u32[]{:S(2)}) collective-permute-start(f32[3,8,1,128]{3,1,2,0:T(8,128)S(1)} %slice.498), channel_id=1, source_target_pairs={{0,2},{1,3},{4,6},{5,7},{8,10},{9,11},{12,14},{13,15},{16,18},{17,... | collective-permute-start | bytes 36872 | tf_op jit(solution)/shard_map/ppermute | solution.py:20
  32.7 18.4 %collective-permute-start.2 = (f32[4,1,36,2]{3,0,2,1:T(4,128)S(1)}, f32[4,1,36,2]{3,0,2,1:T(4,128)S(1)}, u32[]{:S(2)}, u32[]{:S(2)}) collective-permute-start(f32[4,1,36,2]{3,0,2,1:T(4,128)S(1)} %get-tuple-element.87), channel_id=1, source_target_pairs={{0,4},{4,8},{8,12},{12,0},{1,5},{5,9},{9,13},{13,1},{2,6},{6,10},{... | collective-permute-start | bytes 3464 | tf_op jit(solution)/shard_map/ppermute | solution.py:20
  34.3 16.8 %collective-permute-start.3 = (f32[4,1,36,2]{3,0,2,1:T(4,128)S(1)}, f32[4,1,36,2]{3,0,2,1:T(4,128)S(1)}, u32[]{:S(2)}, u32[]{:S(2)}) collective-permute-start(f32[4,1,36,2]{3,0,2,1:T(4,128)S(1)} %get-tuple-element.88), channel_id=1, source_target_pairs={{4,0},{8,4},{12,8},{0,12},{5,1},{9,5},{13,9},{1,13},{6,2},{10,6},{... | collective-permute-start | bytes 3464 | tf_op jit(solution)/shard_map/ppermute | solution.py:21
  51.9 10.6 %collective-permute-start.6 = (f32[3,8,34,1]{3,1,2,0:T(8,128)S(1)}, f32[3,8,34,1]{3,1,2,0:T(8,128)S(1)}, u32[]{:S(2)}, u32[]{:S(2)}) collective-permute-start(f32[3,8,34,1]{3,1,2,0:T(8,128)S(1)} %get-tuple-element.44), channel_id=1, source_target_pairs={{0,4},{4,8},{8,12},{12,0},{1,5},{5,9},{9,13},{13,1},{2,6},{6,10},{... | collective-permute-start | bytes 9800 | tf_op jit(solution)/shard_map/ppermute | solution.py:20
  52.0 13.1 %collective-permute-start.7 = (f32[3,8,34,1]{3,1,2,0:T(8,128)S(1)}, f32[3,8,34,1]{3,1,2,0:T(8,128)S(1)}, u32[]{:S(2)}, u32[]{:S(2)}) collective-permute-start(f32[3,8,34,1]{3,1,2,0:T(8,128)S(1)} %get-tuple-element.45), channel_id=1, source_target_pairs={{4,0},{8,4},{12,8},{0,12},{5,1},{9,5},{13,9},{1,13},{6,2},{10,6},{... | collective-permute-start | bytes 9800 | tf_op jit(solution)/shard_map/ppermute | solution.py:21
  66.1 16.5 %collective-permute-start.9 = (f32[1,8,1,128]{3,2,1,0:T(1,128)S(1)}, f32[1,8,1,128]{3,2,1,0:T(1,128)S(1)}, u32[]{:S(2)}, u32[]{:S(2)}) collective-permute-start(f32[1,8,1,128]{3,2,1,0:T(1,128)S(1)} %get-tuple-element.86), channel_id=1, source_target_pairs={{2,0},{3,1},{6,4},{7,5},{10,8},{11,9},{14,12},{15,13},{18,16},{19,... | collective-permute-start | bytes 12296 | tf_op jit(solution)/shard_map/ppermute | solution.py:21
  67.4 15.2 %collective-permute-start.8 = (f32[1,8,1,128]{3,2,1,0:T(1,128)S(1)}, f32[1,8,1,128]{3,2,1,0:T(1,128)S(1)}, u32[]{:S(2)}, u32[]{:S(2)}) collective-permute-start(f32[1,8,1,128]{3,2,1,0:T(1,128)S(1)} %get-tuple-element.85), channel_id=1, source_target_pairs={{0,2},{1,3},{4,6},{5,7},{8,10},{9,11},{12,14},{13,15},{16,18},{17,... | collective-permute-start | bytes 12296 | tf_op jit(solution)/shard_map/ppermute | solution.py:20
  82.8 7.1 %collective-permute-start.10 = (f32[1,8,34,1]{3,1,2,0:T(8,128)S(1)}, f32[1,8,34,1]{3,1,2,0:T(8,128)S(1)}, u32[]{:S(2)}, u32[]{:S(2)}) collective-permute-start(f32[1,8,34,1]{3,1,2,0:T(8,128)S(1)} %get-tuple-element.75), channel_id=1, source_target_pairs={{0,4},{4,8},{8,12},{12,0},{1,5},{5,9},{9,13},{13,1},{2,6},{6,10},{... | collective-permute-start | bytes 3272 | tf_op jit(solution)/shard_map/ppermute | solution.py:20
  82.8 7.0 %collective-permute-start.11 = (f32[1,8,34,1]{3,1,2,0:T(8,128)S(1)}, f32[1,8,34,1]{3,1,2,0:T(8,128)S(1)}, u32[]{:S(2)}, u32[]{:S(2)}) collective-permute-start(f32[1,8,34,1]{3,1,2,0:T(8,128)S(1)} %get-tuple-element.76), channel_id=1, source_target_pairs={{4,0},{8,4},{12,8},{0,12},{5,1},{9,5},{13,9},{1,13},{6,2},{10,6},{... | collective-permute-start | bytes 3272 | tf_op jit(solution)/shard_map/ppermute | solution.py:21
  90.6 23.2 %collective-permute-start.13 = (f32[3,8,1,128]{3,2,1,0:T(1,128)S(1)}, f32[3,8,1,128]{3,2,1,0:T(1,128)S(1)}, u32[]{:S(2)}, u32[]{:S(2)}) collective-permute-start(f32[3,8,1,128]{3,2,1,0:T(1,128)S(1)} %get-tuple-element.53), channel_id=1, source_target_pairs={{2,0},{3,1},{6,4},{7,5},{10,8},{11,9},{14,12},{15,13},{18,16},{19,... | collective-permute-start | bytes 36872 | tf_op jit(solution)/shard_map/ppermute | solution.py:21
  91.9 22.0 %collective-permute-start.12 = (f32[3,8,1,128]{3,2,1,0:T(1,128)S(1)}, f32[3,8,1,128]{3,2,1,0:T(1,128)S(1)}, u32[]{:S(2)}, u32[]{:S(2)}) collective-permute-start(f32[3,8,1,128]{3,2,1,0:T(1,128)S(1)} %get-tuple-element.52), channel_id=1, source_target_pairs={{0,2},{1,3},{4,6},{5,7},{8,10},{9,11},{12,14},{13,15},{16,18},{17,... | collective-permute-start | bytes 36872 | tf_op jit(solution)/shard_map/ppermute | solution.py:20
  114.2 10.1 %collective-permute-start.14 = (f32[3,8,34,1]{3,1,2,0:T(8,128)S(1)}, f32[3,8,34,1]{3,1,2,0:T(8,128)S(1)}, u32[]{:S(2)}, u32[]{:S(2)}) collective-permute-start(f32[3,8,34,1]{3,1,2,0:T(8,128)S(1)} %get-tuple-element.42), channel_id=1, source_target_pairs={{0,4},{4,8},{8,12},{12,0},{1,5},{5,9},{9,13},{13,1},{2,6},{6,10},{... | collective-permute-start | bytes 9800 | tf_op jit(solution)/shard_map/ppermute | solution.py:20
  114.2 12.7 %collective-permute-start.15 = (f32[3,8,34,1]{3,1,2,0:T(8,128)S(1)}, f32[3,8,34,1]{3,1,2,0:T(8,128)S(1)}, u32[]{:S(2)}, u32[]{:S(2)}) collective-permute-start(f32[3,8,34,1]{3,1,2,0:T(8,128)S(1)} %get-tuple-element.43), channel_id=1, source_target_pairs={{4,0},{8,4},{12,8},{0,12},{5,1},{9,5},{13,9},{1,13},{6,2},{10,6},{... | collective-permute-start | bytes 9800 | tf_op jit(solution)/shard_map/ppermute | solution.py:21
  128.0 16.2 %collective-permute-start.17 = (f32[1,8,1,128]{3,2,1,0:T(1,128)S(1)}, f32[1,8,1,128]{3,2,1,0:T(1,128)S(1)}, u32[]{:S(2)}, u32[]{:S(2)}) collective-permute-start(f32[1,8,1,128]{3,2,1,0:T(1,128)S(1)} %get-tuple-element.84), channel_id=1, source_target_pairs={{2,0},{3,1},{6,4},{7,5},{10,8},{11,9},{14,12},{15,13},{18,16},{19,... | collective-permute-start | bytes 12296 | tf_op jit(solution)/shard_map/ppermute | solution.py:21
  129.3 14.9 %collective-permute-start.16 = (f32[1,8,1,128]{3,2,1,0:T(1,128)S(1)}, f32[1,8,1,128]{3,2,1,0:T(1,128)S(1)}, u32[]{:S(2)}, u32[]{:S(2)}) collective-permute-start(f32[1,8,1,128]{3,2,1,0:T(1,128)S(1)} %get-tuple-element.83), channel_id=1, source_target_pairs={{0,2},{1,3},{4,6},{5,7},{8,10},{9,11},{12,14},{13,15},{16,18},{17,... | collective-permute-start | bytes 12296 | tf_op jit(solution)/shard_map/ppermute | solution.py:20
  144.3 6.9 %collective-permute-start.18 = (f32[1,8,34,1]{3,1,2,0:T(8,128)S(1)}, f32[1,8,34,1]{3,1,2,0:T(8,128)S(1)}, u32[]{:S(2)}, u32[]{:S(2)}) collective-permute-start(f32[1,8,34,1]{3,1,2,0:T(8,128)S(1)} %get-tuple-element.73), channel_id=1, source_target_pairs={{0,4},{4,8},{8,12},{12,0},{1,5},{5,9},{9,13},{13,1},{2,6},{6,10},{... | collective-permute-start | bytes 3272 | tf_op jit(solution)/shard_map/ppermute | solution.py:20
  144.5 6.7 %collective-permute-start.19 = (f32[1,8,34,1]{3,1,2,0:T(8,128)S(1)}, f32[1,8,34,1]{3,1,2,0:T(8,128)S(1)}, u32[]{:S(2)}, u32[]{:S(2)}) collective-permute-start(f32[1,8,34,1]{3,1,2,0:T(8,128)S(1)} %get-tuple-element.74), channel_id=1, source_target_pairs={{4,0},{8,4},{12,8},{0,12},{5,1},{9,5},{13,9},{1,13},{6,2},{10,6},{... | collective-permute-start | bytes 3272 | tf_op jit(solution)/shard_map/ppermute | solution.py:21
  152.0 20.6 %collective-permute-start.21 = (f32[3,8,1,128]{3,2,1,0:T(1,128)S(1)}, f32[3,8,1,128]{3,2,1,0:T(1,128)S(1)}, u32[]{:S(2)}, u32[]{:S(2)}) collective-permute-start(f32[3,8,1,128]{3,2,1,0:T(1,128)S(1)} %get-tuple-element.51), channel_id=1, source_target_pairs={{2,0},{3,1},{6,4},{7,5},{10,8},{11,9},{14,12},{15,13},{18,16},{19,... | collective-permute-start | bytes 36872 | tf_op jit(solution)/shard_map/ppermute | solution.py:21
  153.3 19.4 %collective-permute-start.20 = (f32[3,8,1,128]{3,2,1,0:T(1,128)S(1)}, f32[3,8,1,128]{3,2,1,0:T(1,128)S(1)}, u32[]{:S(2)}, u32[]{:S(2)}) collective-permute-start(f32[3,8,1,128]{3,2,1,0:T(1,128)S(1)} %get-tuple-element.50), channel_id=1, source_target_pairs={{0,2},{1,3},{4,6},{5,7},{8,10},{9,11},{12,14},{13,15},{16,18},{17,... | collective-permute-start | bytes 36872 | tf_op jit(solution)/shard_map/ppermute | solution.py:20
  172.9 11.4 %collective-permute-start.22 = (f32[3,8,34,1]{3,1,2,0:T(8,128)S(1)}, f32[3,8,34,1]{3,1,2,0:T(8,128)S(1)}, u32[]{:S(2)}, u32[]{:S(2)}) collective-permute-start(f32[3,8,34,1]{3,1,2,0:T(8,128)S(1)} %get-tuple-element.40), channel_id=1, source_target_pairs={{0,4},{4,8},{8,12},{12,0},{1,5},{5,9},{9,13},{13,1},{2,6},{6,10},{... | collective-permute-start | bytes 9800 | tf_op jit(solution)/shard_map/ppermute | solution.py:20
  175.0 15.3 %collective-permute-start.23 = (f32[3,8,34,1]{3,1,2,0:T(8,128)S(1)}, f32[3,8,34,1]{3,1,2,0:T(8,128)S(1)}, u32[]{:S(2)}, u32[]{:S(2)}) collective-permute-start(f32[3,8,34,1]{3,1,2,0:T(8,128)S(1)} %get-tuple-element.41), channel_id=1, source_target_pairs={{4,0},{8,4},{12,8},{0,12},{5,1},{9,5},{13,9},{1,13},{6,2},{10,6},{... | collective-permute-start | bytes 9800 | tf_op jit(solution)/shard_map/ppermute | solution.py:21
  191.3 16.4 %collective-permute-start.25 = (f32[1,8,1,128]{3,2,1,0:T(1,128)S(1)}, f32[1,8,1,128]{3,2,1,0:T(1,128)S(1)}, u32[]{:S(2)}, u32[]{:S(2)}) collective-permute-start(f32[1,8,1,128]{3,2,1,0:T(1,128)S(1)} %get-tuple-element.82), channel_id=1, source_target_pairs={{2,0},{3,1},{6,4},{7,5},{10,8},{11,9},{14,12},{15,13},{18,16},{19,... | collective-permute-start | bytes 12296 | tf_op jit(solution)/shard_map/ppermute | solution.py:21
  192.6 15.1 %collective-permute-start.24 = (f32[1,8,1,128]{3,2,1,0:T(1,128)S(1)}, f32[1,8,1,128]{3,2,1,0:T(1,128)S(1)}, u32[]{:S(2)}, u32[]{:S(2)}) collective-permute-start(f32[1,8,1,128]{3,2,1,0:T(1,128)S(1)} %get-tuple-element.81), channel_id=1, source_target_pairs={{0,2},{1,3},{4,6},{5,7},{8,10},{9,11},{12,14},{13,15},{16,18},{17,... | collective-permute-start | bytes 12296 | tf_op jit(solution)/shard_map/ppermute | solution.py:20
  207.8 8.5 %collective-permute-start.26 = (f32[1,8,34,1]{3,1,2,0:T(8,128)S(1)}, f32[1,8,34,1]{3,1,2,0:T(8,128)S(1)}, u32[]{:S(2)}, u32[]{:S(2)}) collective-permute-start(f32[1,8,34,1]{3,1,2,0:T(8,128)S(1)} %get-tuple-element.71), channel_id=1, source_target_pairs={{0,4},{4,8},{8,12},{12,0},{1,5},{5,9},{9,13},{13,1},{2,6},{6,10},{... | collective-permute-start | bytes 3272 | tf_op jit(solution)/shard_map/ppermute | solution.py:20
  207.9 11.1 %collective-permute-start.27 = (f32[1,8,34,1]{3,1,2,0:T(8,128)S(1)}, f32[1,8,34,1]{3,1,2,0:T(8,128)S(1)}, u32[]{:S(2)}, u32[]{:S(2)}) collective-permute-start(f32[1,8,34,1]{3,1,2,0:T(8,128)S(1)} %get-tuple-element.72), channel_id=1, source_target_pairs={{4,0},{8,4},{12,8},{0,12},{5,1},{9,5},{13,9},{1,13},{6,2},{10,6},{... | collective-permute-start | bytes 3272 | tf_op jit(solution)/shard_map/ppermute | solution.py:21
  219.7 20.2 %collective-permute-start.29 = (f32[3,8,1,128]{3,2,1,0:T(1,128)S(1)}, f32[3,8,1,128]{3,2,1,0:T(1,128)S(1)}, u32[]{:S(2)}, u32[]{:S(2)}) collective-permute-start(f32[3,8,1,128]{3,2,1,0:T(1,128)S(1)} %get-tuple-element.49), channel_id=1, source_target_pairs={{2,0},{3,1},{6,4},{7,5},{10,8},{11,9},{14,12},{15,13},{18,16},{19,... | collective-permute-start | bytes 36872 | tf_op jit(solution)/shard_map/ppermute | solution.py:21
  221.0 19.0 %collective-permute-start.28 = (f32[3,8,1,128]{3,2,1,0:T(1,128)S(1)}, f32[3,8,1,128]{3,2,1,0:T(1,128)S(1)}, u32[]{:S(2)}, u32[]{:S(2)}) collective-permute-start(f32[3,8,1,128]{3,2,1,0:T(1,128)S(1)} %get-tuple-element.48), channel_id=1, source_target_pairs={{0,2},{1,3},{4,6},{5,7},{8,10},{9,11},{12,14},{13,15},{16,18},{17,... | collective-permute-start | bytes 36872 | tf_op jit(solution)/shard_map/ppermute | solution.py:20
  240.3 10.1 %collective-permute-start.30 = (f32[3,8,34,1]{3,1,2,0:T(8,128)S(1)}, f32[3,8,34,1]{3,1,2,0:T(8,128)S(1)}, u32[]{:S(2)}, u32[]{:S(2)}) collective-permute-start(f32[3,8,34,1]{3,1,2,0:T(8,128)S(1)} %get-tuple-element.38), channel_id=1, source_target_pairs={{0,4},{4,8},{8,12},{12,0},{1,5},{5,9},{9,13},{13,1},{2,6},{6,10},{... | collective-permute-start | bytes 9800 | tf_op jit(solution)/shard_map/ppermute | solution.py:20
  240.4 12.7 %collective-permute-start.31 = (f32[3,8,34,1]{3,1,2,0:T(8,128)S(1)}, f32[3,8,34,1]{3,1,2,0:T(8,128)S(1)}, u32[]{:S(2)}, u32[]{:S(2)}) collective-permute-start(f32[3,8,34,1]{3,1,2,0:T(8,128)S(1)} %get-tuple-element.39), channel_id=1, source_target_pairs={{4,0},{8,4},{12,8},{0,12},{5,1},{9,5},{13,9},{1,13},{6,2},{10,6},{... | collective-permute-start | bytes 9800 | tf_op jit(solution)/shard_map/ppermute | solution.py:21
  254.1 16.4 %collective-permute-start.33 = (f32[1,8,1,128]{3,2,1,0:T(1,128)S(1)}, f32[1,8,1,128]{3,2,1,0:T(1,128)S(1)}, u32[]{:S(2)}, u32[]{:S(2)}) collective-permute-start(f32[1,8,1,128]{3,2,1,0:T(1,128)S(1)} %get-tuple-element.80), channel_id=1, source_target_pairs={{2,0},{3,1},{6,4},{7,5},{10,8},{11,9},{14,12},{15,13},{18,16},{19,... | collective-permute-start | bytes 12296 | tf_op jit(solution)/shard_map/ppermute | solution.py:21
  255.4 15.1 %collective-permute-start.32 = (f32[1,8,1,128]{3,2,1,0:T(1,128)S(1)}, f32[1,8,1,128]{3,2,1,0:T(1,128)S(1)}, u32[]{:S(2)}, u32[]{:S(2)}) collective-permute-start(f32[1,8,1,128]{3,2,1,0:T(1,128)S(1)} %get-tuple-element.79), channel_id=1, source_target_pairs={{0,2},{1,3},{4,6},{5,7},{8,10},{9,11},{12,14},{13,15},{16,18},{17,... | collective-permute-start | bytes 12296 | tf_op jit(solution)/shard_map/ppermute | solution.py:20
  270.6 7.1 %collective-permute-start.34 = (f32[1,8,34,1]{3,1,2,0:T(8,128)S(1)}, f32[1,8,34,1]{3,1,2,0:T(8,128)S(1)}, u32[]{:S(2)}, u32[]{:S(2)}) collective-permute-start(f32[1,8,34,1]{3,1,2,0:T(8,128)S(1)} %get-tuple-element.69), channel_id=1, source_target_pairs={{0,4},{4,8},{8,12},{12,0},{1,5},{5,9},{9,13},{13,1},{2,6},{6,10},{... | collective-permute-start | bytes 3272 | tf_op jit(solution)/shard_map/ppermute | solution.py:20
  272.6 6.4 %collective-permute-start.35 = (f32[1,8,34,1]{3,1,2,0:T(8,128)S(1)}, f32[1,8,34,1]{3,1,2,0:T(8,128)S(1)}, u32[]{:S(2)}, u32[]{:S(2)}) collective-permute-start(f32[1,8,34,1]{3,1,2,0:T(8,128)S(1)} %get-tuple-element.70), channel_id=1, source_target_pairs={{4,0},{8,4},{12,8},{0,12},{5,1},{9,5},{13,9},{1,13},{6,2},{10,6},{... | collective-permute-start | bytes 3272 | tf_op jit(solution)/shard_map/ppermute | solution.py:21
  279.8 20.2 %collective-permute-start.37 = (f32[3,8,1,128]{3,2,1,0:T(1,128)S(1)}, f32[3,8,1,128]{3,2,1,0:T(1,128)S(1)}, u32[]{:S(2)}, u32[]{:S(2)}) collective-permute-start(f32[3,8,1,128]{3,2,1,0:T(1,128)S(1)} %get-tuple-element.47), channel_id=1, source_target_pairs={{2,0},{3,1},{6,4},{7,5},{10,8},{11,9},{14,12},{15,13},{18,16},{19,... | collective-permute-start | bytes 36872 | tf_op jit(solution)/shard_map/ppermute | solution.py:21
  281.1 19.0 %collective-permute-start.36 = (f32[3,8,1,128]{3,2,1,0:T(1,128)S(1)}, f32[3,8,1,128]{3,2,1,0:T(1,128)S(1)}, u32[]{:S(2)}, u32[]{:S(2)}) collective-permute-start(f32[3,8,1,128]{3,2,1,0:T(1,128)S(1)} %get-tuple-element.46), channel_id=1, source_target_pairs={{0,2},{1,3},{4,6},{5,7},{8,10},{9,11},{12,14},{13,15},{16,18},{17,... | collective-permute-start | bytes 36872 | tf_op jit(solution)/shard_map/ppermute | solution.py:20
  300.4 10.0 %collective-permute-start.38 = (f32[3,8,34,1]{3,1,2,0:T(8,128)S(1)}, f32[3,8,34,1]{3,1,2,0:T(8,128)S(1)}, u32[]{:S(2)}, u32[]{:S(2)}) collective-permute-start(f32[3,8,34,1]{3,1,2,0:T(8,128)S(1)} %get-tuple-element.36), channel_id=1, source_target_pairs={{0,4},{4,8},{8,12},{12,0},{1,5},{5,9},{9,13},{13,1},{2,6},{6,10},{... | collective-permute-start | bytes 9800 | tf_op jit(solution)/shard_map/ppermute | solution.py:20
  300.9 12.5 %collective-permute-start.39 = (f32[3,8,34,1]{3,1,2,0:T(8,128)S(1)}, f32[3,8,34,1]{3,1,2,0:T(8,128)S(1)}, u32[]{:S(2)}, u32[]{:S(2)}) collective-permute-start(f32[3,8,34,1]{3,1,2,0:T(8,128)S(1)} %get-tuple-element.37), channel_id=1, source_target_pairs={{4,0},{8,4},{12,8},{0,12},{5,1},{9,5},{13,9},{1,13},{6,2},{10,6},{... | collective-permute-start | bytes 9800 | tf_op jit(solution)/shard_map/ppermute | solution.py:21
  314.4 16.2 %collective-permute-start.41 = (f32[1,8,1,128]{3,2,1,0:T(1,128)S(1)}, f32[1,8,1,128]{3,2,1,0:T(1,128)S(1)}, u32[]{:S(2)}, u32[]{:S(2)}) collective-permute-start(f32[1,8,1,128]{3,2,1,0:T(1,128)S(1)} %get-tuple-element.78), channel_id=1, source_target_pairs={{2,0},{3,1},{6,4},{7,5},{10,8},{11,9},{14,12},{15,13},{18,16},{19,... | collective-permute-start | bytes 12296 | tf_op jit(solution)/shard_map/ppermute | solution.py:21
  315.7 14.9 %collective-permute-start.40 = (f32[1,8,1,128]{3,2,1,0:T(1,128)S(1)}, f32[1,8,1,128]{3,2,1,0:T(1,128)S(1)}, u32[]{:S(2)}, u32[]{:S(2)}) collective-permute-start(f32[1,8,1,128]{3,2,1,0:T(1,128)S(1)} %get-tuple-element.77), channel_id=1, source_target_pairs={{0,2},{1,3},{4,6},{5,7},{8,10},{9,11},{12,14},{13,15},{16,18},{17,... | collective-permute-start | bytes 12296 | tf_op jit(solution)/shard_map/ppermute | solution.py:20
  330.8 6.9 %collective-permute-start.42 = (f32[1,8,34,1]{3,1,2,0:T(8,128)S(1)}, f32[1,8,34,1]{3,1,2,0:T(8,128)S(1)}, u32[]{:S(2)}, u32[]{:S(2)}) collective-permute-start(f32[1,8,34,1]{3,1,2,0:T(8,128)S(1)} %get-tuple-element.67), channel_id=1, source_target_pairs={{0,4},{4,8},{8,12},{12,0},{1,5},{5,9},{9,13},{13,1},{2,6},{6,10},{... | collective-permute-start | bytes 3272 | tf_op jit(solution)/shard_map/ppermute | solution.py:20
  331.0 6.7 %collective-permute-start.43 = (f32[1,8,34,1]{3,1,2,0:T(8,128)S(1)}, f32[1,8,34,1]{3,1,2,0:T(8,128)S(1)}, u32[]{:S(2)}, u32[]{:S(2)}) collective-permute-start(f32[1,8,34,1]{3,1,2,0:T(8,128)S(1)} %get-tuple-element.68), channel_id=1, source_target_pairs={{4,0},{8,4},{12,8},{0,12},{5,1},{9,5},{13,9},{1,13},{6,2},{10,6},{... | collective-permute-start | bytes 3272 | tf_op jit(solution)/shard_map/ppermute | solution.py:21
where the time goes:
time: 340 us; the launch traced here: 339 us
  blocking collectives  131 us (39%)
  starting transfers between devices  107 us (31%)
  waiting for transfers between devices  70.6 us (21%)
  local copies, waits for them, and re-layouts  18.5 us (5%)
  other arithmetic  10.8 us (3%)
    all_gather x11, blocking collectives, extend(): whole_rows = lax.all_gather(edge_rows, 'lon', axis=3, tiled=True)  131 us
    ppermute x22, starting transfers between devices, with_halo(): before = lax.ppermute(last, axis, up)  57.1 us
    ppermute x22, starting transfers between devices, with_halo(): after = lax.ppermute(first, axis, down)  50.2 us
    ppermute x22, waiting for transfers between devices, with_halo(): before = lax.ppermute(last, axis, up)  49.7 us
    ppermute x22, waiting for transfers between devices, with_halo(): after = lax.ppermute(first, axis, down)  20.9 us
    gather x21, local copies, waits for them, and re-layouts, extend(): mirror = jnp.take(whole_rows, facing, axis=3) * signs  8.4 us
  transfers between devices with their start and end apart: 44, of which 17 were waited for; matrix products, arithmetic and copies ran while one was open for 4% of the time, Pallas kernels for 0%

commit v1 on v0

v1 whole, which is shorter than its diff:
```python
import functools
from collections import deque

import jax
import jax.numpy as jnp
from jax import lax
from jax.experimental import pallas as pl
from jax.experimental.pallas import tpu as pltpu
from jax.sharding import PartitionSpec as P

SUBCYCLES = 5
NLEV = 90
TIME_STEP = 0.35
HALF_STEP = 0.5 * TIME_STEP

LANES = 128
SUBLANES = 8
HALF = LANES // 2
HALO = 2 * SUBCYCLES
PAIRS = HALO // 2
FIELDS = 4
STATE = 3
COEF = 3
STRIP_SLOTS = HALF // HALO
CORNER_SLOTS = LANES // (2 * HALO)
F32 = jnp.float32


def ceil_div(a, b):
    return -(-a // b)


class Shapes:
    def __init__(self, height):
        self.height = height
        self.ext = height + 2 * HALO
        self.mid = self.ext // 2
        self.fold_first = height
        self.blocks = FIELDS * PAIRS
        self.strip_rows = height // 2
        self.strips = ceil_div(self.strip_rows * FIELDS, STRIP_SLOTS)
        self.side = self.blocks + self.strips
        self.main = STATE * HALO + PAIRS
        self.corners = ceil_div(FIELDS * HALO, CORNER_SLOTS)
        self.band = self.main + self.corners

    def strip(self, k, f):
        slot = (k - HALO) * FIELDS + f
        return self.blocks + slot // STRIP_SLOTS, HALO * (slot % STRIP_SLOTS)

    def corner(self, i, f):
        slot = f * HALO + i
        return self.main + slot // CORNER_SLOTS, 2 * HALO * (slot % CORNER_SLOTS)


def roll(x, shift, axis=1):
    shift = shift % x.shape[axis]
    return x if shift == 0 else pltpu.roll(x, shift, axis)


def lane_ids():
    return lax.broadcasted_iota(jnp.int32, (SUBLANES, LANES), 1)


def sublane_ids():
    return lax.broadcasted_iota(jnp.int32, (SUBLANES, LANES), 0)


def run_staged(tasks, window):
    waiting = deque()

    def advance(task):
        try:
            next(task)
        except StopIteration:
            return
        waiting.append(task)

    for task in tasks:
        advance(task)
        while len(waiting) >= window:
            advance(waiting.popleft())
    while waiting:
        advance(waiting.popleft())


def own_row(x_ref, c_ref, height, f, row):
    if f == COEF:
        return c_ref[row]
    return x_ref[f, pl.ds(row, SUBLANES, stride=height), :]


def pick_pair(even, first, second):
    return jnp.where(even, first, second)


def fold_place(fold_ref, lon_size):
    pivot = fold_ref[0]
    block = pivot // LANES
    rest = pivot - block * LANES
    low = rest < HALF
    place = jnp.where(low, rest + LANES, rest)
    branch = jnp.where(low, block - 1 + lon_size, block)
    return lax.rem(branch, lon_size), place


def sides_kernel(sh, sizes, x_ref, b_ref, m_ref, l_ref, p_ref, a_out, b_out, c_out, q_out):
    lat_size, lon_size = sizes
    height = sh.height
    q_out[0], _ = fold_place(p_ref, lon_size)

    wet = m_ref[...].astype(F32)
    depth = 0.5 + 1.5 * ((l_ref[...] - 1).astype(F32) / (NLEV - 1)) ** 2
    row0 = lax.axis_index("lat") * height
    rows = (row0 + lax.broadcasted_iota(jnp.int32, (height, LANES), 0)).astype(F32)
    coriolis = 0.3 + 0.2 * rows / (height * lat_size)
    planes = (
        HALF_STEP * (wet * (depth + b_ref[0])),
        HALF_STEP * b_ref[1],
        HALF_STEP * b_ref[2],
        wet * (TIME_STEP * coriolis),
    )
    c_out[...] = jnp.zeros_like(c_out)
    for c, plane in enumerate(planes):
        for r in range(height):
            c_out[r, c : c + 1, :] = plane[r : r + 1, :]

    even = jnp.full((SUBLANES, LANES), lax.rem(lax.axis_index("lon"), 2), jnp.int32) == 0
    lane = lane_ids()
    low = lane < HALF
    own = functools.partial(own_row, x_ref, c_out, height)
    top = height - HALO

    def block(f, i):
        a, b = own(f, top + i), own(f, top + i + PAIRS)
        a_up, b_up = roll(a, HALF), roll(b, HALF)
        yield
        east = jnp.where(low, a_up, b)
        west = jnp.where(low, a, b_up)
        v = f * PAIRS + i
        a_out[v] = jnp.where(even, east, west)
        b_out[v] = jnp.where(even, west, east)

    slots = {}
    for k in range(HALO, sh.mid):
        for f in range(FIELDS):
            v, at = sh.strip(k, f)
            slots.setdefault(v, []).append((k, f, at))

    def strips(v):
        parts = []
        for k, f, at in slots[v]:
            a, b = own(f, k - HALO), own(f, sh.ext - 1 - k - HALO)
            beyond = HALF if sh.ext - 1 - k >= sh.fold_first else 0
            parts.append(
                (
                    at,
                    roll(a, at - (LANES - HALO)),
                    roll(b, HALF + at - (LANES - HALO) + beyond),
                    roll(a, at),
                    roll(b, HALF + at - beyond),
                )
            )
        yield
        east = west = jnp.zeros((SUBLANES, LANES), F32)
        for at, ea, eb, wa, wb in parts:
            here = (lane >= at) & (lane < at + HALO)
            there = (lane >= HALF + at) & (lane < HALF + at + HALO)
            east = jnp.where(here, ea, jnp.where(there, eb, east))
            west = jnp.where(here, wa, jnp.where(there, wb, west))
        a_out[v] = jnp.where(even, east, west)
        b_out[v] = jnp.where(even, west, east)

    run_staged([block(f, i) for f in range(FIELDS) for i in range(PAIRS)], 10)
    run_staged([strips(v) for v in sorted(slots)], 2)


def bands_kernel(sh, sizes, x_ref, c_ref, ra_ref, rb_ref, p_ref, *outs):
    lat_size, lon_size = sizes
    height = sh.height
    fold_out, lat_outs = outs[0], outs[1:]
    even = jnp.full((SUBLANES, LANES), lax.rem(lax.axis_index("lon"), 2), jnp.int32) == 0
    lane, sub = lane_ids(), sublane_ids()
    low = lane < HALF
    own = functools.partial(own_row, x_ref, c_ref, height)
    top = height - HALO

    def from_east(v):
        return jnp.where(even, ra_ref[v], rb_ref[v])

    def from_west(v):
        return jnp.where(even, rb_ref[v], ra_ref[v])

    def pair_coefs(a, b):
        return jnp.where(sub < SUBLANES // 2, a, roll(b, SUBLANES // 2, 0))

    corner_items = {}
    for f in range(FIELDS):
        for i in range(HALO):
            v, at = sh.corner(i, f)
            corner_items.setdefault(v, []).append((i, f, at))

    def band(out, first, is_top):
        def main():
            for f in range(STATE):
                for i in range(HALO):
                    out[f * HALO + i] = own(f, first + i)
            for i in range(PAIRS):
                out[STATE * HALO + i] = pair_coefs(
                    own(COEF, first + i), own(COEF, first + i + PAIRS)
                )

        def corners(v):
            parts = []
            for i, f, at in corner_items[v]:
                if is_top:
                    src, h = f * PAIRS + i % PAIRS, HALF * (i // PAIRS)
                    w_at, e_at = h + HALF - HALO, h
                else:
                    src, w_at = sh.strip(HALO + i, f)
                    e_at = w_at
                parts.append(
                    (at, roll(from_west(src), at - w_at), roll(from_east(src), at + HALO - e_at))
                )
            yield
            total = jnp.zeros((SUBLANES, LANES), F32)
            for at, w, e in parts:
                total = jnp.where((lane >= at) & (lane < at + HALO), w, total)
                total = jnp.where((lane >= at + HALO) & (lane < at + 2 * HALO), e, total)
            out[v] = total

        main()
        run_staged([corners(v) for v in sorted(corner_items)], 3)

    lat_even = lax.rem(lax.axis_index("lat"), 2) == 0

    @pl.when(lat_even)
    def _():
        band(lat_outs[0], top, True)
        if lat_size > 2:
            band(lat_outs[1], 0, False)

    @pl.when(jnp.logical_not(lat_even))
    def _():
        band(lat_outs[0], 0, False)
        if lat_size > 2:
            band(lat_outs[1], top, True)

    @pl.when(lax.axis_index("lat") == lat_size - 1)
    def _():
        _, place = fold_place(p_ref, lon_size)
        where_to = jnp.full((SUBLANES, LANES), place, jnp.int32)
        rest = where_to & (LANES - 1)
        eastern = where_to >= LANES
        backwards = (where_to - lane) & (LANES - 1)
        main_own = (eastern & (lane >= rest + 1)) | (jnp.logical_not(eastern) & (lane <= rest))
        upper = (lane >= rest + 1) & (lane <= rest + HALO)
        lower = (lane >= rest + 1 - HALO) & (lane <= rest)
        side_own = (eastern & lower) | (jnp.logical_not(eastern) & upper)
        side_far = (eastern & upper & (lane >= HALF)) | (
            jnp.logical_not(eastern) & lower & (lane < HALF)
        )
        coef_signs = jnp.where((sub == 1) | (sub == 2), -1.0, 1.0).astype(F32)

        def reversed_row(f, i):
            v, h = f * PAIRS + i % PAIRS, i // PAIRS
            w, e = from_west(v), from_east(v)
            if h == 0:
                w = roll(w, HALF)
            else:
                e = roll(e, HALF)
            v, at = sh.strip(sh.ext - 1 - sh.fold_first - i, f)
            far_w = roll(from_west(v), HALF - HALO - HALF - at)
            far_e = roll(from_east(v), -at)
            yield
            both = jnp.where(low, e, w)
            mine = own(f, top + i)
            main = jnp.where(main_own, mine, both)
            side = jnp.where(
                side_own, mine, jnp.where(side_far, jnp.where(low, far_w, far_e), both)
            )
            if f == COEF:
                main, side = main * coef_signs, side * coef_signs
            elif f > 0:
                main, side = -main, -side
            main = jnp.take_along_axis(main, backwards, axis=1)
            side = jnp.take_along_axis(side, backwards, axis=1)
            yield
            j = HALO - 1 - i
            v, at = sh.corner(j, f)
            side = roll(side, at - (LANES - HALO))
            if f < STATE:
                fold_out[f * HALO + j] = main
            elif j < PAIRS:
                v2 = STATE * HALO + j
                fold_out[v2] = jnp.where(sub < SUBLANES // 2, main, fold_out[v2])
            else:
                fold_out[STATE * HALO + j - PAIRS] = roll(main, SUBLANES // 2, 0)
            yield
            here = (lane >= at) & (lane < at + 2 * HALO)
            fold_out[v] = jnp.where(here, side, fold_out[v])

        for v in range(STATE * HALO, sh.band):
            fold_out[v] = jnp.zeros((SUBLANES, LANES), F32)
        run_staged([reversed_row(f, i) for f in range(FIELDS) for i in range(HALO)], 8)


def steps_kernel(sh, sizes, has_second, *refs):
    lat_size, lon_size = sizes
    x_ref, c_ref, ra_ref, rb_ref, fold_ref, lat_a = refs[:6]
    lat_b = refs[6] if has_second else None
    out_ref, main, main_c, edge, edge_c = refs[7 if has_second else 6 :]
    height, ext, mid = sh.height, sh.ext, sh.mid
    even = jnp.full((SUBLANES, LANES), lax.rem(lax.axis_index("lon"), 2), jnp.int32) == 0
    lane, sub = lane_ids(), sublane_ids()
    low = lane < HALF
    own = functools.partial(own_row, x_ref, c_ref, height)

    def from_east(v):
        return jnp.where(even, ra_ref[v], rb_ref[v])

    def from_west(v):
        return jnp.where(even, rb_ref[v], ra_ref[v])

    def put_main(f, r, value):
        if f == COEF:
            main_c[r] = value
        else:
            main[f, r] = value

    def get_main(f, r):
        return main_c[r] if f == COEF else main[f, r]

    def add_edge(f, k, value, mask):
        if f == COEF:
            edge_c[k] = jnp.where(mask, value, edge_c[k])
        else:
            edge[f, k] = jnp.where(mask, value, edge[f, k])

    east0 = HALF // 2
    half_lane = lane & (HALF - 1)
    west_halo = half_lane < HALO
    west_own = (half_lane >= HALO) & (half_lane < 3 * HALO)
    east_own = (half_lane >= east0) & (half_lane < east0 + 2 * HALO)
    east_halo = (half_lane >= east0 + 2 * HALO) & (half_lane < east0 + 3 * HALO)

    def take_band(ref, north):
        def rows(f, i):
            r = (sh.ext - HALO + i) if north else i
            if f < STATE:
                put_main(f, r, ref[f * HALO + i])
            else:
                v = ref[STATE * HALO + i % PAIRS]
                put_main(f, r, v if i < PAIRS else roll(v, SUBLANES // 2, 0))
            v, at = sh.corner(i, f)
            base = HALF if north else 0
            w = roll(ref[v], base - at)
            e = roll(ref[v], base + east0 + HALO - at)
            yield
            k = sh.ext - 1 - r if north else r
            value = jnp.where(half_lane < HALO, w, e)
            if f == COEF:
                edge_c[k, :, base : base + HALF] = value[:, base : base + HALF]
            else:
                edge[f, k, :, base : base + HALF] = value[:, base : base + HALF]

        run_staged([rows(f, i) for f in range(FIELDS) for i in range(HALO)], 10)

    def no_band():
        zero = jnp.zeros((SUBLANES, LANES), F32)
        for f in range(FIELDS):
            for i in range(HALO):
                put_main(f, i, zero)
                if f == COEF:
                    edge_c[i, :, :HALF] = zero[:, :HALF]
                else:
                    edge[f, i, :, :HALF] = zero[:, :HALF]

    lat = lax.axis_index("lat")
    lat_even = lax.rem(lat, 2) == 0
    at_top = lat == lat_size - 1

    @pl.when(at_top)
    def _():
        take_band(fold_ref, True)

    @pl.when(jnp.logical_not(at_top) & lat_even)
    def _():
        take_band(lat_a, True)

    @pl.when(jnp.logical_not(lat_even))
    def _():
        take_band(lat_a, False)

    @pl.when(lat == 0)
    def _():
        no_band()

    if has_second:

        @pl.when(jnp.logical_not(at_top) & jnp.logical_not(lat_even))
        def _():
            take_band(lat_b, True)

        @pl.when((lat > 0) & lat_even)
        def _():
            take_band(lat_b, False)

    for f in range(FIELDS):
        for r in range(height):
            put_main(f, HALO + r, own(f, r))

    def edge_rows(f, k):
        a, b = get_main(f, k), get_main(f, ext - 1 - k)
        aw, ae = roll(a, HALO), roll(a, east0 - (LANES - 2 * HALO))
        bw, be = roll(b, HALF + HALO), roll(b, HALF + east0 - (LANES - 2 * HALO))
        if k >= HALO:
            v, at = sh.strip(k, f)
            w, e = roll(from_west(v), -at), roll(from_east(v), east0 + 2 * HALO - at)
            if ext - 1 - k >= sh.fold_first:
                i = ext - 1 - k - sh.fold_first
                v, h = f * PAIRS + i % PAIRS, HALF * (i // PAIRS)
                w2 = roll(from_west(v), HALF - (h + HALF - HALO))
                e2 = roll(from_east(v), HALF + east0 + 2 * HALO - h)
            else:
                w2 = e2 = None
        yield
        value = jnp.where(east_own, jnp.where(low, ae, be), jnp.where(low, aw, bw))
        if k >= HALO:
            if w2 is not None:
                w, e = jnp.where(low, w, w2), jnp.where(low, e, e2)
            value = jnp.where(west_halo, w, value)
            value = jnp.where(east_halo, e, value)
        else:
            mine = west_own | east_own
            halo = edge_c[k] if f == COEF else edge[f, k]
            value = jnp.where(mine, value, halo)
        if f == COEF:
            edge_c[k] = value
        else:
            edge[f, k] = value

    run_staged([edge_rows(f, k) for f in range(FIELDS) for k in range(mid)], 6)

    north_sign = jnp.where(low, 1.0, -1.0).astype(F32)
    for r in range(ext):
        main_c[r, 4:5, :] = jnp.where(main_c[r, 0:1, :] > 0, 1.0, 0.0).astype(F32)
    for k in range(mid):
        thick = edge_c[k, 0:1, :]
        edge_c[k, 4:5, :] = jnp.where(thick > 0, 1.0, 0.0).astype(F32)
        edge_c[k, 5:6, :] = thick * north_sign[0:1]
        edge_c[k, 2:3, :] = edge_c[k, 2:3, :] * north_sign[0:1]

    def coef(ref, r, c):
        return jnp.broadcast_to(ref[r, c : c + 1, :], (SUBLANES, LANES))

    class Sweep:
        def __init__(self, step, state, coefs, count, mirrored, final):
            self.state, self.coefs, self.count = state, coefs, count
            self.mirrored, self.final = mirrored, final
            self.lo = 2 * step - 1
            self.hi = count if mirrored else count - self.lo
            self.flux_n, self.rolled, self.elev, self.slopes = {}, {}, {}, {}
            self.step_n = HALF_STEP * north_sign if mirrored else HALF_STEP

        def flux(self, r):
            s, c = self.state, self.coefs
            eta, zonal, merid = s[0, r], s[1, r], s[2, r]
            thick = coef(c, r, 0)
            thick_n = coef(c, r, 5) if self.mirrored else thick
            self.flux_n[r] = thick_n * merid + coef(c, r, 2) * eta
            if self.lo <= r < self.hi:
                east = thick * zonal + coef(c, r, 1) * eta
                self.rolled[r] = (roll(east, -1), roll(east, 1))
            if self.mirrored and r == self.count - 1:
                self.flux_n[r + 1] = -roll(self.flux_n[r], HALF)

        def elevation(self, r):
            if not self.lo <= r < self.hi:
                return
            plus, minus = self.rolled.pop(r)
            change = (plus - minus) + (self.flux_n[r + 1] - self.flux_n[r - 1])
            eta = coef(self.coefs, r, 4) * (self.state[0, r] - change)
            self.elev[r] = eta
            if self.velocity_row(r):
                if not self.final:
                    self.state[0, r] = eta
                self.slopes[r] = (roll(eta, -1), roll(eta, 1))
            if self.mirrored and r == self.count - 1:
                self.elev[r + 1] = roll(eta, HALF)

        def velocity_row(self, r):
            return self.lo < r < (self.hi if self.mirrored else self.hi - 1)

        def velocity(self, r):
            if not self.velocity_row(r):
                return
            plus, minus = self.slopes.pop(r)
            wet, turn = coef(self.coefs, r, 4), coef(self.coefs, r, 3)
            zonal, merid = self.state[1, r], self.state[2, r]
            zonal = wet * (zonal - HALF_STEP * (plus - minus)) + turn * merid
            slope = self.step_n * (self.elev[r + 1] - self.elev[r - 1])
            merid = wet * (merid - slope) - turn * zonal
            if self.final:
                self.final(r, (self.elev[r], zonal, merid))
            else:
                self.state[1, r] = zonal
                self.state[2, r] = merid
            self.elev.pop(r - 1)

        def advance(self, t, lag):
            if self.lo - 1 <= t < (self.hi if self.mirrored else self.hi + 1):
                self.flux(t)
            self.elevation(t - lag)
            self.velocity(t - 2 * lag)

    def keep_edge(k, values):
        for f in range(STATE):
            edge[f, k] = values[f]

    pending = deque()

    def emit(limit):
        while len(pending) > limit:
            r, values, moved = pending.popleft()
            for f in range(STATE):
                w, e = moved[f]
                value = jnp.where(lane < HALO, w, jnp.where(lane >= LANES - HALO, e, values[f]))
                out_ref[f, pl.ds(r - HALO, SUBLANES, stride=height), :] = value

    def write_row(r, values):
        k, h = (r, 0) if r < mid else (ext - 1 - r, HALF)
        moved = []
        for f in range(STATE):
            v = edge[f, k]
            moved.append(
                (
                    roll(v, -(h + HALO)),
                    roll(v, LANES - HALO - (h + east0 + HALO)),
                )
            )
        pending.append((r, values, moved))
        emit(3)

    lag = 5
    for step in range(1, SUBCYCLES + 1):
        last = step == SUBCYCLES
        edges = Sweep(step, edge, edge_c, mid, True, keep_edge if last else None)
        rows = Sweep(step, main, main_c, ext, False, write_row if last else None)
        if last:
            for t in range(mid + 2 * lag):
                edges.advance(t, lag)
            for t in range(ext + 2 * lag):
                rows.advance(t, lag)
            emit(0)
        else:
            for t in range(ext + 2 * lag):
                rows.advance(t, lag)
                if t % 2 == 0:
                    edges.advance(t // 2, lag)
            for t in range((ext + 2 * lag + 1) // 2, mid + 2 * lag):
                edges.advance(t, lag)


def pair_swaps(size, wrap):
    first = [(i, i ^ 1) for i in range(size)]
    second = []
    for i in range(size):
        j = i + 1 if i % 2 else i - 1
        if wrap or 0 <= j < size:
            second.append((i, j % size))
    return first, second


def vmem(n):
    return [pl.BlockSpec(memory_space=pltpu.VMEM)] * n


def smem():
    return pl.BlockSpec(memory_space=pltpu.SMEM)


def on_device(mesh_sizes, perturb, background, land_mask, levels, fold_partner):
    lat_size, lon_size = mesh_sizes
    height = perturb.shape[2]
    sh = Shapes(height)
    sizes = (lat_size, lon_size)
    flat = perturb.reshape(STATE, SUBLANES * height, LANES)
    tile = (SUBLANES, LANES)

    def shape(n):
        return jax.ShapeDtypeStruct((n,) + tile, F32)

    params = pltpu.CompilerParams(vmem_limit_bytes=32 * 1024 * 1024)
    side_a, side_b, coefs, branch = pl.pallas_call(
        functools.partial(sides_kernel, sh, sizes),
        out_shape=(
            shape(sh.side),
            shape(sh.side),
            shape(height),
            jax.ShapeDtypeStruct((1,), jnp.int32),
        ),
        in_specs=vmem(4) + [smem()],
        out_specs=tuple(vmem(3)) + (smem(),),
        compiler_params=params,
        name="sides",
    )(flat, background, land_mask, levels, fold_partner)

    lon_first, lon_second = pair_swaps(lon_size, True)
    got_a = lax.ppermute(side_a, "lon", lon_first)
    got_b = lax.ppermute(side_b, "lon", lon_second)

    n_lat = 1 if lat_size == 2 else 2
    bands = pl.pallas_call(
        functools.partial(bands_kernel, sh, sizes),
        out_shape=tuple(shape(sh.band) for _ in range(1 + n_lat)),
        in_specs=vmem(4) + [smem()],
        out_specs=tuple(vmem(1 + n_lat)),
        compiler_params=params,
        name="bands",
    )(flat, coefs, got_a, got_b, fold_partner)

    lat_swaps = pair_swaps(lat_size, False)[:n_lat]
    top = lat_size - 1

    def exchange(q, bands):
        across = []
        for m in range(lon_size):
            j = (q - m) % lon_size
            across.append((m * lat_size + top, j * lat_size + top))
        got = [lax.ppermute(band, "lat", pairs) for band, pairs in zip(bands[1:], lat_swaps)]
        got.insert(0, lax.ppermute(bands[0], ("lon", "lat"), across))
        return tuple(got)

    got = lax.switch(
        branch[0], [functools.partial(exchange, q) for q in range(lon_size)], bands
    )

    out = pl.pallas_call(
        functools.partial(steps_kernel, sh, sizes, n_lat == 2),
        out_shape=jax.ShapeDtypeStruct(flat.shape, F32),
        in_specs=vmem(5 + n_lat),
        out_specs=vmem(1)[0],
        scratch_shapes=[
            pltpu.VMEM((STATE, sh.ext) + tile, F32),
            pltpu.VMEM((sh.ext,) + tile, F32),
            pltpu.VMEM((STATE, sh.mid) + tile, F32),
            pltpu.VMEM((sh.mid,) + tile, F32),
        ],
        compiler_params=params,
        name="subcycles",
    )(flat, coefs, got_a, got_b, *got)
    return out.reshape(perturb.shape)


def solution(mesh):
    placed = (
        P("grp", "dir", "lat", "lon"),
        P("grp", "lat", "lon"),
        P("lat", "lon"),
        P("lat", "lon"),
        P(),
    )
    sizes = (mesh.shape["lat"], mesh.shape["lon"])
    return jax.shard_map(
        functools.partial(on_device, sizes),
        mesh=mesh,
        in_specs=placed,
        out_specs=P("grp", "dir", "lat", "lon"),
        check_vma=False,
    )
```

time: 340 us -> 33.5 us (0.10)
  the two profiles are of different devices: /device:TPU:0 before, /device:TPU:18 now
where the time goes in v1:
time: 33.5 us; the launch traced here: 33.2 us
  waiting for transfers between devices  15.6 us (47%)
  Pallas kernels  9.03 us (27%)
  local copies, waits for them, and re-layouts  3.91 us (12%)
  starting transfers between devices  3.91 us (12%)
  between operations  0.68 us (2%)
    ppermute x1, waiting for transfers between devices, exchange(): got.insert(0, lax.ppermute(bands[0], ('lon', 'lat'), across))  8.64 us
    pallas_call x1, Pallas kernels, on_device(): pl.pallas_call(functools.partial(steps_kernel, sh, sizes, n_lat == 2), ou...  6.32 us
    ppermute x1, waiting for transfers between devices, on_device(): got_a = lax.ppermute(side_a, 'lon', lon_first)  4.06 us
    unnamed x12, local copies, waits for them, and re-layouts  3.91 us
    ppermute x1, waiting for transfers between devices, on_device(): got_b = lax.ppermute(side_b, 'lon', lon_second)  2.87 us
    ppermute x1, starting transfers between devices, exchange(): got.insert(0, lax.ppermute(bands[0], ('lon', 'lat'), across))  2.19 us
    ppermute x1, starting transfers between devices, on_device(): got_a = lax.ppermute(side_a, 'lon', lon_first)  1.64 us
    pallas_call x1, Pallas kernels, on_device(): pl.pallas_call(functools.partial(sides_kernel, sh, sizes), out_shape=(sha...  1.43 us
  transfers between devices with their start and end apart: 4, of which 3 were waited for; matrix products, arithmetic and copies ran while one was open for 0% of the time, Pallas kernels for 0%

profile of v1, /device:TPU:18, one launch (start us, length us, event | category | flops | bytes accessed | tf_op | source)
XLA Modules:
  0.0 33.2 jit_solution(16871773142499886238)
XLA Ops:
  0.0 0.0 copy-start
  0.0 1.0 %copy-done = f32[3,8,32,128]{3,2,1,0:T(8,128)S(1)} copy-done((f32[3,8,32,128]{3,2,1,0:T(8,128)S(1)}, f32[3,8,32,128]{3,2,1,0:T(8,128)}, u32[]{:S(2)}) %copy-start) | copy-done | bytes 393240
  1.0 0.0 copy-start.2
  1.0 0.8 %copy-done.2 = f32[3,32,128]{2,1,0:T(8,128)S(1)} copy-done((f32[3,32,128]{2,1,0:T(8,128)S(1)}, f32[3,32,128]{2,1,0:T(8,128)}, u32[]{:S(2)}) %copy-start.2) | copy-done | bytes 49176
  1.8 0.0 copy-start.3
  1.8 0.7 %copy-done.3 = s32[32,128]{1,0:T(8,128)S(1)} copy-done((s32[32,128]{1,0:T(8,128)S(1)}, s32[32,128]{1,0:T(8,128)}, u32[]{:S(2)}) %copy-start.3) | copy-done | bytes 16408
  2.5 0.0 copy-start.4
  2.5 0.7 %copy-done.4 = s32[32,128]{1,0:T(8,128)S(1)} copy-done((s32[32,128]{1,0:T(8,128)S(1)}, s32[32,128]{1,0:T(8,128)}, u32[]{:S(2)}) %copy-start.4) | copy-done | bytes 16408
  3.2 0.0 copy-start.5
  3.2 0.7 %copy-done.5 = s32[512]{0:T(512)S(1)} copy-done((s32[512]{0:T(512)S(1)}, s32[512]{0:T(512)}, u32[]{:S(2)}) %copy-start.5) | copy-done | bytes 2072
  3.9 1.4 %sides.1 = (f32[31,8,128]{2,1,0:T(8,128)S(1)}, f32[31,8,128]{2,1,0:T(8,128)S(1)}, f32[32,8,128]{2,1,0:T(8,128)S(1)}, s32[1]{0:T(128)}) custom-call(f32[3,256,128]{2,1,0:T(8,128)S(1)} %bitcast.3, f32[3,32,128]{2,1,0:T(8,128)S(1)} %copy-done.2, s32[32,128]{1,0:T(8,128)S(1)} %copy-done.3, s32[32,128]{1,0:T(8,128)S(1)} %copy-done.4, s32[512]{0:T(512)S(1)} %copy-done.5), custom_call_target="tpu_custom_call" | custom-call | tf_op jit(solution)/shard_map/sides/pallas_call | solution.py:595
  5.4 1.6 %collective-permute-start.8 = (f32[31,8,128]{2,1,0:T(8,128)S(1)}, f32[31,8,128]{2,1,0:T(8,128)S(1)}, u32[]{:S(2)}, u32[]{:S(2)}) collective-permute-start(f32[31,8,128]{2,1,0:T(8,128)S(1)} %get-tuple-element.36), channel_id=1, source_target_pairs={{0,4},{4,0},{8,12},{12,8},{1,5},{5,1},{9,13},{13,9},{2,6},{6,2},{1... | collective-permute-start | bytes 380936 | tf_op jit(solution)/shard_map/ppermute | solution.py:610
  7.0 0.0 collective-permute-start.9
  7.7 4.1 %collective-permute-done.8.ra_ref.refs_2_ = f32[31,8,128]{2,1,0:T(8,128)S(1)} collective-permute-done((f32[31,8,128]{2,1,0:T(8,128)S(1)}, f32[31,8,128]{2,1,0:T(8,128)S(1)}, u32[]{:S(2)}, u32[]{:S(2)}) %collective-permute-start.8) | collective-permute-done | bytes 127008 | tf_op jit(solution)/shard_map/ppermute | solution.py:610
  11.7 2.9 %collective-permute-done.9.rb_ref.refs_3_ = f32[31,8,128]{2,1,0:T(8,128)S(1)} collective-permute-done((f32[31,8,128]{2,1,0:T(8,128)S(1)}, f32[31,8,128]{2,1,0:T(8,128)S(1)}, u32[]{:S(2)}, u32[]{:S(2)}) %collective-permute-start.9) | collective-permute-done | bytes 127008 | tf_op jit(solution)/shard_map/ppermute | solution.py:611
  14.6 0.0 copy-start.1
  14.6 1.3 %bands.1 = (f32[42,8,128]{2,1,0:T(8,128)S(1)}, f32[42,8,128]{2,1,0:T(8,128)S(1)}) custom-call(f32[3,256,128]{2,1,0:T(8,128)S(1)} %bitcast.4, f32[32,8,128]{2,1,0:T(8,128)S(1)} %get-tuple-element.35.c_ref.refs_1_, f32[31,8,128]{2,1,0:T(8,128)S(1)} %collective-permute-done.8.ra_ref.refs_2_, f32[31,8,128]{2,1,0:T(8,128)S(1)} %collective-permute-done.9.rb_ref.refs_3_, ...), custom_call_target="tpu_custom_call" | custom-call | tf_op jit(solution)/shard_map/bands/pallas_call | solution.py:614
  15.9 11.0 %conditional.1 = (f32[42,8,128]{2,1,0:T(8,128)}, f32[42,8,128]{2,1,0:T(8,128)}) conditional(s32[]{:T(128)} %bitcast.1, (f32[42,8,128]{2,1,0:T(8,128)S(1)}, f32[42,8,128]{2,1,0:T(8,128)S(1)}) %bands.1, (f32[42,8,128]{2,1,0:T(8,128)S(1)}, f32[42,8,128]{2,1,0:T(8,128)S(1)}) %bands.1, (f32[42,8,128]{2,1,0:T(8,128)S(1)}, ...), branch_computations={%region_0.0_spmd, %region_1.0_spmd, %region_2.0_spmd, %region_3.0_... | conditional | bytes 1376352 | solution.py:635
  15.9 2.2 %collective-permute-start.6 = (f32[42,8,128]{2,1,0:T(8,128)S(1)}, f32[42,8,128]{2,1,0:T(8,128)}, u32[]{:S(2)}, u32[]{:S(2)}) collective-permute-start(f32[42,8,128]{2,1,0:T(8,128)S(1)} %get-tuple-element.27), channel_id=1, source_target_pairs={{2,14},{6,10},{10,6},{14,2},{3,15},{7,11},{11,7},{15,3},{18,30},{2... | collective-permute-start | bytes 516104 | tf_op jit(solution)/shard_map/cond/branch_3_fun/ppermute | solution.py:632
  18.1 0.1 collective-permute-start.7
  18.2 8.6 %collective-permute-done.6 = f32[42,8,128]{2,1,0:T(8,128)} collective-permute-done((f32[42,8,128]{2,1,0:T(8,128)S(1)}, f32[42,8,128]{2,1,0:T(8,128)}, u32[]{:S(2)}, u32[]{:S(2)}) %collective-permute-start.6) | collective-permute-done | bytes 172064 | tf_op jit(solution)/shard_map/cond/branch_3_fun/ppermute | solution.py:632
  26.8 0.0 collective-permute-done.7
  26.8 0.0 copy-done.1
  26.8 6.3 %subcycles.1 = f32[3,256,128]{2,1,0:T(8,128)} custom-call(f32[3,256,128]{2,1,0:T(8,128)S(1)} %bitcast.5, f32[32,8,128]{2,1,0:T(8,128)S(1)} %get-tuple-element.35.c_ref.refs_1_, f32[31,8,128]{2,1,0:T(8,128)S(1)} %collective-permute-done.8.ra_ref.refs_2_, f32[31,8,128]{2,1,0:T(8,128)S(1)} %collective-permute-done.9.rb_ref.refs_3_, ...), custom_call_target="tpu_custom_call" | custom-call | tf_op jit(solution)/shard_map/subcycles/pallas_call | solution.py:639
Async XLA Ops:
  0.0 1.0 %copy-start = (f32[3,8,32,128]{3,2,1,0:T(8,128)S(1)}, f32[3,8,32,128]{3,2,1,0:T(8,128)}, u32[]{:S(2)}) copy-start(f32[3,8,32,128]{3,2,1,0:T(8,128)} %param.9) | copy-start | bytes 1179652
  1.0 0.8 %copy-start.2 = (f32[3,32,128]{2,1,0:T(8,128)S(1)}, f32[3,32,128]{2,1,0:T(8,128)}, u32[]{:S(2)}) copy-start(f32[3,32,128]{2,1,0:T(8,128)} %b_ref.1) | copy-start | bytes 147460
  1.8 0.7 %copy-start.3 = (s32[32,128]{1,0:T(8,128)S(1)}, s32[32,128]{1,0:T(8,128)}, u32[]{:S(2)}) copy-start(s32[32,128]{1,0:T(8,128)} %m_ref.1) | copy-start | bytes 49156
  2.5 0.7 %copy-start.4 = (s32[32,128]{1,0:T(8,128)S(1)}, s32[32,128]{1,0:T(8,128)}, u32[]{:S(2)}) copy-start(s32[32,128]{1,0:T(8,128)} %l_ref.1) | copy-start | bytes 49156
  3.2 0.7 %copy-start.5 = (s32[512]{0:T(512)S(1)}, s32[512]{0:T(512)}, u32[]{:S(2)}) copy-start(s32[512]{0:T(512)} %p_ref.3) | copy-start | bytes 6148
  5.4 6.4 %collective-permute-start.8 = (f32[31,8,128]{2,1,0:T(8,128)S(1)}, f32[31,8,128]{2,1,0:T(8,128)S(1)}, u32[]{:S(2)}, u32[]{:S(2)}) collective-permute-start(f32[31,8,128]{2,1,0:T(8,128)S(1)} %get-tuple-element.36), channel_id=1, source_target_pairs={{0,4},{4,0},{8,12},{12,8},{1,5},{5,1},{9,13},{13,9},{2,6},{6,2},{1... | collective-permute-start | bytes 380936 | tf_op jit(solution)/shard_map/ppermute | solution.py:610
  7.0 7.6 %collective-permute-start.9 = (f32[31,8,128]{2,1,0:T(8,128)S(1)}, f32[31,8,128]{2,1,0:T(8,128)S(1)}, u32[]{:S(2)}, u32[]{:S(2)}) collective-permute-start(f32[31,8,128]{2,1,0:T(8,128)S(1)} %get-tuple-element.37), channel_id=1, source_target_pairs={{0,12},{4,8},{8,4},{12,0},{1,13},{5,9},{9,5},{13,1},{2,14},{6,10},... | collective-permute-start | bytes 380936 | tf_op jit(solution)/shard_map/ppermute | solution.py:611
  14.6 12.2 %copy-start.1 = (f32[3,8,32,128]{3,2,1,0:T(8,128)S(1)}, f32[3,8,32,128]{3,2,1,0:T(8,128)}, u32[]{:S(2)}) copy-start(f32[3,8,32,128]{3,2,1,0:T(8,128)} %param.9) | copy-start | bytes 1179652
  15.9 10.9 %collective-permute-start.6 = (f32[42,8,128]{2,1,0:T(8,128)S(1)}, f32[42,8,128]{2,1,0:T(8,128)}, u32[]{:S(2)}, u32[]{:S(2)}) collective-permute-start(f32[42,8,128]{2,1,0:T(8,128)S(1)} %get-tuple-element.27), channel_id=1, source_target_pairs={{2,14},{6,10},{10,6},{14,2},{3,15},{7,11},{11,7},{15,3},{18,30},{2... | collective-permute-start | bytes 516104 | tf_op jit(solution)/shard_map/cond/branch_3_fun/ppermute | solution.py:632
  18.1 8.7 %collective-permute-start.7 = (f32[42,8,128]{2,1,0:T(8,128)S(1)}, f32[42,8,128]{2,1,0:T(8,128)}, u32[]{:S(2)}, u32[]{:S(2)}) collective-permute-start(f32[42,8,128]{2,1,0:T(8,128)S(1)} %get-tuple-element.28), channel_id=1, source_target_pairs={{0,2},{2,0},{1,3},{3,1},{4,6},{6,4},{5,7},{7,5},{8,10},{10,8},{9,1... | collective-permute-start | bytes 516104 | tf_op jit(solution)/shard_map/cond/branch_3_fun/ppermute | solution.py:631
